TPU v7x, 512 devices: a whole 4x8x8 slice. The times are simulated.
512 devices in a mesh: dp: 8 (over z), tensor: 4 (over y_lo, core), grid: 16 (over y_hi, x).
Axes of the slice: x: 4, y: 8 (y_hi: 4, y_lo: 2; y = y_hi * 2 + y_lo), z: 8, core: 2. Of those that a mesh axis runs over, the one named last changes fastest.
Arguments:
- tokens: bfloat16 [6144, 8192], P('dp', 'grid'), may hold values from -6 to 6
- cotangents: bfloat16 [2, 6144, 1024], P(None, 'dp', 'tensor'), may hold values from -0.015625 to 0.015625
- left_stat: float32 [2, 8192, 8192], P(None, ('dp', 'tensor'), 'grid'), may hold values from -6 to 6
- right_stat: float32 [2, 1024, 1024], P(None, ('dp', 'tensor'), 'grid'), may hold values from -6 to 6
- left_root: bfloat16 [2, 8192, 8192], P(None, ('dp', 'tensor'), 'grid'), may hold values from -0.3125 to 0.3125
- right_root: bfloat16 [2, 1024, 1024], P(None, 'grid'), as said below
- momentum: float32 [2, 8192, 1024], P(None, ('dp', 'tensor', 'grid')), may hold values from -6 to 6
Outputs:
- new_left: float32 [2, 8192, 8192], P(None, ('dp', 'tensor'), 'grid')
- new_right: float32 [2, 1024, 1024], P(None, ('dp', 'tensor'), 'grid')
- new_momentum: float32 [2, 8192, 1024], P(None, ('dp', 'tensor', 'grid'))
Inputs may be any that keep to these rules, and one draw needn't show every extreme that they name: `right_root`: each of the two factors is exactly symmetric.
All inputs are finite; a program needn't handle non-finite values.
Results may differ from a plain program's by a relative error of at most 0.0023.
Values may be sent and summed in bfloat16 or wider, within the bound.
A program may use at most 64 MiB of HBM per device.

v0:
```python
import jax
import jax.numpy as jnp
from jax import lax
from jax.sharding import PartitionSpec as P

stat_decay = 0.9
momentum_decay = 0.9


def in_blocks(shard, dim, size):
    dims = shard.shape
    pieces = shard.reshape(*dims[:dim], size, dims[dim] // size, *dims[dim + 1 :])
    return jnp.moveaxis(pieces, dim, 0)


def sum_at_owner(shard, axis, dim):
    size = lax.axis_size(axis)
    pieces = lax.all_to_all(in_blocks(shard, dim, size), axis, 0, 0, tiled=True)
    return jnp.sum(pieces, axis=0)


def rows_for(lines, size):
    spare = -lines.shape[0] % size
    if not spare:
        return lines
    return jnp.concatenate([lines, jnp.zeros((spare, *lines.shape[1:]), lines.dtype)])


def spread(shard, axis, root):
    lines = jnp.where(lax.axis_index(axis) == root, shard, jnp.zeros_like(shard)).reshape(
        -1, *shard.shape[1:][-1:]
    )
    padded = rows_for(lines, lax.axis_size(axis))
    own = lax.psum_scatter(padded, axis, scatter_dimension=0, tiled=True)
    return lax.all_gather(own, axis, axis=0, tiled=True)[: len(lines)].reshape(shard.shape)


def shards(tokens, cotangents, left_stat, right_stat, left_root, right_root, momentum):
    partial_grad = jnp.einsum("tr,pto->pro", tokens, cotangents, preferred_element_type=jnp.float32)
    shared = sum_at_owner(partial_grad, "dp", 1)
    widened = lax.all_gather(shared.astype(jnp.bfloat16), "tensor", axis=2, tiled=True)
    grad_rows = lax.all_gather(widened, "dp", axis=1, tiled=True)
    block_rows = left_stat.shape[1]
    grid_rows = left_stat.shape[2]
    learner = lax.axis_index("dp") * lax.axis_size("tensor") + lax.axis_index("tensor")
    first_row = learner * block_rows
    source = first_row // grid_rows
    offset = first_row % grid_rows
    selected = lax.dynamic_slice_in_dim(grad_rows, offset, block_rows, 1)
    own_rows = spread(selected, "grid", source)
    gram_left = jnp.einsum("pak,pbk->pab", own_rows, grad_rows, preferred_element_type=jnp.float32)
    new_left = stat_decay * left_stat + (1.0 - stat_decay) * gram_left
    column_width = right_stat.shape[2]
    column_block = lax.dynamic_slice_in_dim(
        own_rows, lax.axis_index("grid") * column_width, column_width, 2
    )
    right_term = jnp.einsum(
        "pak,pac->pkc", own_rows, column_block, preferred_element_type=jnp.float32
    )
    gram_right = sum_at_owner(right_term, ("dp", "tensor"), 1)
    new_right = stat_decay * right_stat + (1.0 - stat_decay) * gram_right
    applied = sum_at_owner(
        jnp.einsum("pab,pbk->apk", left_root, grad_rows, preferred_element_type=jnp.float32),
        "grid",
        0,
    )
    factor_local = right_root.astype(jnp.float32)
    local_columns = jnp.einsum(
        "mpk,pck->mpc",
        lax.all_gather(applied, "grid", axis=0, tiled=True),
        factor_local,
        precision=lax.Precision.HIGHEST,
        preferred_element_type=jnp.float32,
    )
    update = lax.all_to_all(local_columns, "grid", split_axis=0, concat_axis=2, tiled=True)
    new_momentum = momentum_decay * momentum + jnp.transpose(update, (1, 0, 2))
    return (new_left, new_right, new_momentum)


def solution(mesh):
    return jax.shard_map(
        shards,
        mesh=mesh,
        in_specs=(
            P("dp", "grid"),
            P(None, "dp", "tensor"),
            P(None, ("dp", "tensor"), "grid"),
            P(None, ("dp", "tensor"), "grid"),
            P(None, ("dp", "tensor"), "grid"),
            P(None, "grid", None),
            P(None, ("dp", "tensor", "grid"), None),
        ),
        out_specs=(
            P(None, ("dp", "tensor"), "grid"),
            P(None, ("dp", "tensor"), "grid"),
            P(None, ("dp", "tensor", "grid"), None),
        ),
        check_vma=False,
    )
```

profile of v0, /device:TPU:1, one launch (start us, length us, event | category | flops | bytes accessed | tf_op | source)
XLA Modules:
  0.0 373.7 jit_solution(8418410943962718748)
XLA Ops:
  7.2 1.1 copy-done
  8.3 1.7 convolution_bitcast_fusion
  10.5 37.9 %all_to_all.33 = f32[8,2,64,256]{3,2,1,0:T(8,128)S(1)} all-to-all(f32[8,2,64,256]{3,2,1,0:T(8,128)S(1)} %copy.26), channel_id=1, replica_groups=mesh['dp'=8,'tensor'=4,'grid'=16] {'dp'}, dimensions={0} | all-to-all | bytes 2097152 | tf_op jit(solution)/shard_map/all_to_all | solution.py:18
  48.4 8.7 %all_gather.12 = bf16[2,64,1024]{2,1,0:T(8,128)(2,1)} all-gather(bf16[2,64,256]{2,1,0:T(8,128)(2,1)S(1)} %reduce_sum.27), channel_id=1, replica_groups=mesh['dp'=8,'tensor'=4,'grid'=16] {'tensor'}, dimensions={2}, use_global_device_ids=true | all-gather | bytes 327680 | tf_op jit(solution)/shard_map/all_gather | solution.py:41
  57.3 36.3 %all-gather.4.cloned.1.call-done = bf16[2,512,1024]{2,1,0:T(8,128)(2,1)} async-done(((bf16[2,64,1024]{2,1,0:T(8,128)(2,1)}), bf16[2,512,1024]{2,1,0:T(8,128)(2,1)}) %all-gather.4.cloned.1.call-update) | async-done | bytes 2097168 | tf_op jit(solution)/shard_map/all_gather | solution.py:42
  93.6 2.6 dynamic-slice_select_fusion
  96.9 1.4 copy.30
  98.4 9.0 %all-to-all-start.2 = ((f32[16,16,2,1024]{3,1,2,0:T(8,128)}), f32[16,16,2,1024]{3,1,2,0:T(8,128)}, u32[]{:S(2)}, u32[]{:S(2)}) async-start(f32[16,16,2,1024]{3,1,2,0:T(8,128)} %copy.30), calls=%async_computation.3 | async-start | bytes 4194304 | tf_op jit(solution)/shard_map/all_to_all | solution.py:18
  107.5 110.3 %reduce-scatter.2.cloned.1.call-done = bf16[32,1024]{1,0:T(8,128)(2,1)} async-done(((bf16[512,1024]{1,0:T(8,128)(2,1)}), bf16[32,1024]{1,0:T(8,128)(2,1)}) %reduce-scatter.2.cloned.1.call-update) | async-done | bytes 65552 | tf_op jit(solution)/shard_map/reduce_scatter | solution.py:34
  217.9 2.4 reduce_sum.29
  220.3 58.3 %all-gather.6.cloned.1.call-done = bf16[512,1024]{1,0:T(8,128)(2,1)} async-done(((bf16[32,1024]{1,0:T(8,128)(2,1)}), bf16[512,1024]{1,0:T(8,128)(2,1)}) %all-gather.6.cloned.1.call-update) | async-done | bytes 1048592 | tf_op jit(solution)/shard_map/all_gather | solution.py:35
  278.6 1.8 fusion.2
  280.4 1.1 copy.29
  281.5 2.7 reshape.27
  284.2 9.2 %all-to-all-start.1 = ((f32[32,1,4096]{2,1,0:T(1,128)}), f32[32,1,4096]{2,1,0:T(1,128)S(1)}, u32[]{:S(2)}, u32[]{:S(2)}) async-start(f32[32,1,4096]{2,1,0:T(1,128)} %reshape.27), calls=%async_computation.2 | async-start | bytes 1048576 | tf_op jit(solution)/shard_map/all_to_all | solution.py:18
  293.4 51.5 %all-gather.8.cloned.1.call-done = f32[256,2,1024]{2,0,1:T(8,128)} async-done(((f32[16,2,1024]{2,0,1:T(8,128)}), f32[256,2,1024]{2,0,1:T(8,128)}) %all-gather.8.cloned.1.call-update) | async-done | bytes 2097168 | tf_op jit(solution)/shard_map/all_gather | solution.py:70
  344.9 2.8 convolution_bitcast_fusion.1
  347.7 0.8 copy.31
  348.5 1.9 reshape.29
  350.4 5.4 %all-to-all-start.3 = ((f32[16,1,2048]{2,1,0:T(1,128)}), f32[16,1,2048]{2,1,0:T(1,128)S(1)}, u32[]{:S(2)}, u32[]{:S(2)}) async-start(f32[16,1,2048]{2,1,0:T(1,128)} %reshape.29), calls=%async_computation.4 | async-start | bytes 262144 | tf_op jit(solution)/shard_map/all_to_all | solution.py:75
  355.9 3.3 fusion
  359.7 1.8 reduce
  362.7 2.5 all-to-all-done.3
  365.1 0.9 reduce.1
  (32 shorter events, 4.2 us)
Async XLA Ops:
  7.2 1.1 copy-start
  7.2 86.4 %all-gather.4.cloned.1.call-start = ((), (), s32[]{:S(2)}) async-start(), calls=%async_computation.5 | async-start | bytes 2359296 | tf_op jit(solution)/shard_map/all_gather | solution.py:42
  48.4 47.8 %copy-start.2 = (bf16[2,256,512]{2,1,0:T(8,128)(2,1)S(1)}, bf16[2,256,512]{2,1,0:T(8,128)(2,1)}, u32[]{:S(2)}) copy-start(bf16[2,256,512]{2,1,0:T(8,128)(2,1)} %param.11) | copy-start | bytes 1572868
  57.2 160.6 %reduce-scatter.2.cloned.1.call-start = ((), (), s32[]{:S(2)}) async-start(), calls=%async_computation.6 | async-start | bytes 1114112 | tf_op jit(solution)/shard_map/reduce_scatter | solution.py:34
  93.6 2.6 copy-start.1
  98.4 119.5 %all-to-all-start.2 = ((f32[16,16,2,1024]{3,1,2,0:T(8,128)}), f32[16,16,2,1024]{3,1,2,0:T(8,128)}, u32[]{:S(2)}, u32[]{:S(2)}) async-start(f32[16,16,2,1024]{3,1,2,0:T(8,128)} %copy.30), calls=%async_computation.3 | async-start | bytes 4194304 | tf_op jit(solution)/shard_map/all_to_all | solution.py:18
  107.4 171.2 %all-gather.6.cloned.1.call-start = ((), (), s32[]{:S(2)}) async-start(), calls=%async_computation.7 | async-start | bytes 1114112 | tf_op jit(solution)/shard_map/all_gather | solution.py:35
  217.8 127.1 %all-gather.8.cloned.1.call-start = ((), (), s32[]{:S(2)}) async-start(), calls=%async_computation.8 | async-start | bytes 2228224 | tf_op jit(solution)/shard_map/all_gather | solution.py:70
  284.2 66.3 %all-to-all-start.1 = ((f32[32,1,4096]{2,1,0:T(1,128)}), f32[32,1,4096]{2,1,0:T(1,128)S(1)}, u32[]{:S(2)}, u32[]{:S(2)}) async-start(f32[32,1,4096]{2,1,0:T(1,128)} %reshape.27), calls=%async_computation.2 | async-start | bytes 1048576 | tf_op jit(solution)/shard_map/all_to_all | solution.py:18
  350.4 14.7 %all-to-all-start.3 = ((f32[16,1,2048]{2,1,0:T(1,128)}), f32[16,1,2048]{2,1,0:T(1,128)S(1)}, u32[]{:S(2)}, u32[]{:S(2)}) async-start(f32[16,1,2048]{2,1,0:T(1,128)} %reshape.29), calls=%async_computation.4 | async-start | bytes 262144 | tf_op jit(solution)/shard_map/all_to_all | solution.py:75
  359.2 2.9 copy-start.4
  361.5 4.9 %copy-start.3 = (f32[2,16,1024]{2,1,0:T(8,128)S(1)}, f32[2,16,1024]{2,1,0:T(8,128)}, u32[]{:S(2)}) copy-start(f32[2,16,1024]{2,1,0:T(8,128)} %param.13) | copy-start | bytes 393220
Sparse Core Ops, SparseCore 0:
  57.3 36.2 all-gather.3
  98.3 119.4 reduce-scatter.1
  221.3 57.2 all-gather.5
  282.5 62.4 all-gather.7
where the time goes:
time: 375 us; the launch traced here: 374 us
  waiting for transfers between devices  259 us (69%)
  blocking collectives  46.6 us (12%)
  starting transfers between devices  23.9 us (6%)
  between operations  14 us (4%)
  local copies, waits for them, and re-layouts  10.7 us (3%)
  matrix products  10.4 us (3%)
  other arithmetic  9.07 us (2%)
    reduce_scatter x1, waiting for transfers between devices, spread(): own = lax.psum_scatter(padded, axis, scatter_dimension=0, tiled=True)  110 us
    all_gather x1, waiting for transfers between devices, spread(): lax.all_gather(own, axis, axis=0, tiled=True)[:len(lines)]  58.3 us
    all_gather x1, waiting for transfers between devices, shards(): lax.all_gather(applied, 'grid', axis=0, tiled=True)  51.5 us
    all_to_all x1, blocking collectives, sum_at_owner(): pieces = lax.all_to_all(in_blocks(shard, dim, size), axis, 0, 0, tiled=True)  37.9 us
    all_gather x1, waiting for transfers between devices, shards(): grad_rows = lax.all_gather(widened, 'dp', axis=1, tiled=True)  36.3 us
    all_to_all x2, starting transfers between devices, sum_at_owner(): pieces = lax.all_to_all(in_blocks(shard, dim, size), axis, 0, 0, tiled=True)  18.3 us
    all_gather x1, blocking collectives, shards(): lax.all_gather(shared.astype(jnp.bfloat16), 'tensor', axis=2, tiled=True)  8.74 us
  transfers between devices with their start and end apart: 7, of which 5 were waited for; matrix products, arithmetic and copies ran while one was open for 6% of the time, Pallas kernels for 0%

commit v1 on v0

v1 whole, which is shorter than its diff:
```python
import jax
import jax.numpy as jnp
from jax import lax
from jax.experimental import pallas as pl
from jax.experimental.pallas import tpu as pltpu
from jax.sharding import PartitionSpec as P

MESH = pl.DeviceIdType.MESH
f32, bf16 = jnp.float32, jnp.bfloat16

stat_decay = 0.9
momentum_decay = 0.9

NZ, NT, NG, NX, NY = 8, 4, 16, 4, 4
Z_ORDER = (1, 7, 2, 6, 3, 5, 4)


def remote(src, dst, send_sem, recv_sem, device):
    return pltpu.make_async_remote_copy(
        src_ref=src, dst_ref=dst, send_sem=send_sem, recv_sem=recv_sem,
        device_id=device, device_id_type=MESH,
    )


def kernel(
    tokens, cots, left_root, right_root,
    gram_left, gram_right, update,
    part, ring, gbuf, gsub, r1, r2, r3, rbuf, rr,
    xs, xr, ax, ys, yr, uf, ur, gr_tmp, gs32, gs, gr,
    ring_send, ring_recv, ag_send, ag_recv, sib_send, sib_recv, yl_send, yl_recv,
    sib2_send, sib2_recv, x_send, x_recv, pair_send, pair_recv,
):
    d, t, g = lax.axis_index("dp"), lax.axis_index("tensor"), lax.axis_index("grid")
    y, x = g // NX, g % NX
    core, y_lo = t % 2, t // 2
    sibling = y_lo * 2 + (1 - core)
    partner = (1 - y_lo) * 2 + core
    learner = d * NT + t

    barrier = pltpu.get_barrier_semaphore()

    @pl.loop(1, NZ * NT)
    def _(k):
        other = (learner + k) % (NZ * NT)
        pl.semaphore_signal(barrier, inc=1, device_id=(other // NT, other % NT, g), device_id_type=MESH)

    @pl.loop(1, NG)
    def _(k):
        pl.semaphore_signal(barrier, inc=1, device_id=(d, t, (g + k) % NG), device_id_type=MESH)

    turned = tokens[...].T
    for p in range(2):
        whole = jnp.dot(turned, cots[p], preferred_element_type=f32)
        for z in range(NZ):
            part[z, p] = whole[z * 64 : z * 64 + 64]

    pl.semaphore_wait(barrier, NZ * NT - 1 + NG - 1)

    sent = []

    def go(copy):
        copy.start()
        sent.append(copy)

    up, down = ((d + 1) % NZ, t, g), ((d + NZ - 1) % NZ, t, g)

    def length(way, p):
        return 4 if way == p else 3

    for step in range(4):
        for p in range(2):
            for way in range(2):
                n = length(way, p)
                if step >= n:
                    continue
                e = (d + n - step) % NZ if way == 0 else (d + NZ - n + step) % NZ
                if step == 0:
                    src = part.at[e, p]
                else:
                    slot = ring.at[way, p, step - 1]
                    remote(slot, slot, ring_send.at[way, p, step - 1], ring_recv.at[way, p, step - 1], up).wait_recv()
                    ring[way, p, step - 1] = ring[way, p, step - 1] + part[e, p]
                    src = slot
                go(remote(src, ring.at[way, p, step], ring_send.at[way, p, step], ring_recv.at[way, p, step],
                          up if way == 0 else down))
        if step == 0:
            @pl.loop(0, NY)
            def _(q):
                @pl.when(jnp.logical_or(q != y, x != y))
                def _():
                    remote(right_root.at[core], rr.at[core, pl.ds(x * 64, 64)], pair_send.at[0], pair_recv.at[0],
                           (d, t, q * NX + y)).start()

            @pl.when(x == y)
            def _():
                rr[core, pl.ds(x * 64, 64), :] = right_root[core]

    for p in range(2):
        total = part[d, p]
        for way in range(2):
            n = length(way, p)
            slot = ring.at[way, p, n - 1]
            remote(slot, slot, ring_send.at[way, p, n - 1], ring_recv.at[way, p, n - 1], up).wait_recv()
            total = total + ring[way, p, n - 1]
        piece = total.astype(bf16)
        gbuf[p, t, pl.ds(d * 64, 64), :] = piece
        for a in range(4):
            for c in range(2):
                gsub[p * 8 + a * 2 + c] = piece[a * 16 : a * 16 + 16, c * 128 : c * 128 + 128]

    def rows_of(tensor, k):
        return gbuf.at[:, tensor, pl.ds(((d + NZ - k) % NZ) * 64, 64), :]

    for k in Z_ORDER:
        go(remote(rows_of(t, 0), rows_of(t, 0), ag_send.at[k], ag_recv.at[k], ((d + k) % NZ, t, g)))

    def pass_on(k):
        go(remote(rows_of(t, k), rows_of(t, k), yl_send.at[k], yl_recv.at[k], (d, partner, g)))
        go(remote(rows_of(t, k), rows_of(t, k), sib_send.at[k], sib_recv.at[k], (d, sibling, g)))

    def pass_again(k):
        here = rows_of(partner, k)
        remote(here, here, yl_send.at[k], yl_recv.at[k], (d, partner, g)).wait_recv()
        go(remote(here, here, sib2_send.at[k], sib2_recv.at[k], (d, sibling, g)))

    def arrived(k):
        here = rows_of(t, k)
        remote(here, here, ag_send.at[k], ag_recv.at[k], (d, partner, g)).wait_recv()

    pass_on(0)

    @pl.loop(1, NG)
    def _(k):
        to = (g + k) % NG
        remote(gsub.at[to], r1.at[g], pair_send.at[1], pair_recv.at[1], (d, t, to)).start()

    r1[g] = gsub[g]

    def many(ref, s):
        return remote(ref, ref, pair_send.at[s], pair_recv.at[s], (d, sibling, g))

    for k in (1, 7):
        arrived(k)
        pass_on(k)
    pass_again(0)

    mine = d // 4 == core
    many(r1.at[pl.ds(0, NG - 1)], 1).wait_recv()

    @pl.loop(0, NG)
    def _(b):
        to_z, to_t = b // 2, (b % 2) * 2 + d // 4
        @pl.when(jnp.logical_or(to_z != d, to_t != t))
        def _():
            remote(r1.at[b], r2.at[(d % 4) * NT + t], pair_send.at[2], pair_recv.at[2], (to_z, to_t, g)).start()

    @pl.when(mine)
    def _():
        r2[(d % 4) * NT + t] = r1[2 * d + y_lo]

    for k in (2, 6):
        arrived(k)
        pass_on(k)
    for k in (1, 7):
        pass_again(k)

    @pl.when(mine)
    def _():
        many(r2.at[pl.ds(0, 15)], 2).wait_recv()

    @pl.when(jnp.logical_not(mine))
    def _():
        many(r2, 2).wait_recv()

    for k in range(1, NY):
        go(remote(r2, r3.at[x, y], x_send.at[0, k], x_recv.at[0, k], (d, t, ((y + k) % NY) * NX + x)))
    r3[x, y] = r2[...]

    for k in (3, 5):
        arrived(k)
        pass_on(k)
    for k in (2, 6):
        pass_again(k)

    @pl.when(x == y)
    def _():
        many(rr.at[core, pl.ds(0, 192)], 0).wait_recv()

    @pl.when(x != y)
    def _():
        many(rr.at[core], 0).wait_recv()

    go(remote(rr.at[core], rr.at[core], pair_send.at[3], pair_recv.at[3], (d, sibling, g)))

    arrived(4)
    pass_on(4)
    for k in range(1, NY):
        here = r3.at[x, (y + NY - k) % NY]
        remote(here, here, x_send.at[0, k], x_recv.at[0, k], (d, sibling, g)).wait_recv()
    for k in (2, 1, 3):
        go(remote(r3.at[x], r3.at[x], x_send.at[1, k], x_recv.at[1, k], (d, t, y * NX + (x + k) % NX)))
    for k in (3, 5, 4):
        pass_again(k)
    for k in (0,) + Z_ORDER:
        for tensor, sends, recvs in ((sibling, sib_send, sib_recv), ((1 - y_lo) * 2 + 1 - core, sib2_send, sib2_recv)):
            here = rows_of(tensor, k)
            remote(here, here, sends.at[k], recvs.at[k], (d, sibling, g)).wait_recv()

    for p in range(2):
        for k in (2, 1, 3):
            xs[p, k - 1] = jnp.dot(left_root[p], gbuf[p, (x + k) % NX], preferred_element_type=f32).astype(bf16)
            go(remote(xs.at[p, k - 1], xr.at[p, k - 1], x_send.at[2 + p, k], x_recv.at[2 + p, k],
                      (d, t, y * NX + (x + k) % NX)))
        ax[p] = jnp.dot(left_root[p], gbuf[p, x], preferred_element_type=f32)

    for p in range(2):
        chosen = gbuf[p, d // 2].T
        for j in range(NT):
            gr_tmp[:, j * 256 : j * 256 + 256] = jnp.dot(chosen, gbuf[p, j], preferred_element_type=f32)
        lines = gr_tmp[pl.ds((learner % 8) * 32, 32), :]
        for c in range(8):
            block = lines[:, c * 128 : c * 128 + 128]
            gs32[c, p] = block
            gs[c, p] = block.astype(bf16)

    @pl.loop(1, NG)
    def _(k):
        to = (g + k) % NG
        remote(gs.at[to // 2], gr.at[k - 1], pair_send.at[4], pair_recv.at[4], (d, t, to)).start()

    for p in range(2):
        total = ax[p]
        for k in (1, 3, 2):
            here = xr.at[p, k - 1]
            remote(here, here, x_send.at[2 + p, k], x_recv.at[2 + p, k], (d, sibling, g)).wait_recv()
            total = total + xr[p, k - 1].astype(f32)
        ax[p] = total
        for k in (2, 1, 3):
            to = (y + k) % NY
            ys[p, k - 1] = ax[p, pl.ds(to * 64, 64), :].astype(bf16)
            go(remote(ys.at[p, k - 1], yr.at[p, k - 1], x_send.at[4 + p, k], x_recv.at[4 + p, k], (d, t, to * NX + x)))

    for k in (1, 3, 2):
        here = r3.at[(x + NX - k) % NX]
        remote(here, here, x_send.at[1, k], x_recv.at[1, k], (d, sibling, g)).wait_recv()
    for a in range(NX):
        for b in range(NY):
            p, rows, c = b // 2, (b % 2) * 2 + a // 2, a % 2
            for j in range(NT):
                for z in range(4):
                    rbuf[p, j, z * 64 + rows * 16 : z * 64 + rows * 16 + 16, c * 128 : c * 128 + 128] = r3[a, b, z * NT + j]

    def left(p):
        total = None
        for j in range(NT):
            term = lax.dot_general(rbuf[p, j], gbuf[p, j], (((1,), (1,)), ((), ())), preferred_element_type=f32)
            total = term if total is None else total + term
        gram_left[p] = total

    left(0)

    many(rr.at[1 - core], 3).wait_recv()
    for p in range(2):
        total = ax[p, pl.ds(y * 64, 64), :]
        for k in (1, 3, 2):
            here = yr.at[p, k - 1]
            remote(here, here, x_send.at[4 + p, k], x_recv.at[4 + p, k], (d, sibling, g)).wait_recv()
            total = total + yr[p, k - 1].astype(f32)
        high = total.astype(bf16)
        rest = total - high.astype(f32)
        middle = rest.astype(bf16)
        low = (rest - middle.astype(f32)).astype(bf16)
        product = jnp.dot(jnp.concatenate([high, middle, low]), rr[p], preferred_element_type=f32)
        uf[p] = product[:64] + (product[64:128] + product[128:])
        for k in (2, 1, 3):
            to = (x + k) % NX
            go(remote(uf.at[p, pl.ds(to * 16, 16)], ur.at[p, k - 1], x_send.at[6 + p, k], x_recv.at[6 + p, k],
                      (d, t, y * NX + to)))

    left(1)

    many(gr, 4).wait_recv()
    for p in range(2):
        total = gs32[g // 2, p]
        for k in range(NG - 1):
            total = total + gr[k, p].astype(f32)
        gram_right[p] = jnp.where(g % 2 == 0, total[:, :64], total[:, 64:])

    for p in range(2):
        total = uf[p, pl.ds(x * 16, 16), :]
        for k in (1, 3, 2):
            here = ur.at[p, k - 1]
            remote(here, here, x_send.at[6 + p, k], x_recv.at[6 + p, k], (d, sibling, g)).wait_recv()
            total = total + ur[p, k - 1]
        update[p] = total

    for copy in sent:
        copy.wait_send()
    many(gsub.at[pl.ds(0, NG - 1)], 1).wait_send()
    many(gr, 4).wait_send()

    @pl.when(mine)
    def _():
        many(r2.at[pl.ds(0, 15)], 2).wait_send()

    @pl.when(jnp.logical_not(mine))
    def _():
        many(r2, 2).wait_send()

    @pl.when(x == y)
    def _():
        many(rr.at[core, pl.ds(0, 192)], 0).wait_send()

    @pl.when(x != y)
    def _():
        many(rr.at[core], 0).wait_send()


def shards(tokens, cotangents, left_stat, right_stat, left_root, right_root, momentum):
    vmem = pl.BlockSpec(memory_space=pltpu.VMEM)
    V, S = pltpu.VMEM, pltpu.SemaphoreType.DMA
    gram_left, gram_right, update = pl.pallas_call(
        kernel,
        out_shape=(
            jax.ShapeDtypeStruct((2, 256, 512), f32),
            jax.ShapeDtypeStruct((2, 32, 64), f32),
            jax.ShapeDtypeStruct((2, 16, 1024), f32),
        ),
        in_specs=[vmem] * 4,
        out_specs=(vmem,) * 3,
        scratch_shapes=[
            V((NZ, 2, 64, 256), f32),
            V((2, 2, 4, 64, 256), f32),
            V((2, NT, 512, 256), bf16),
            V((NG, 16, 128), bf16),
            V((NG, 16, 128), bf16),
            V((16, 16, 128), bf16),
            V((NX, NY, 16, 16, 128), bf16),
            V((2, NT, 256, 256), bf16),
            V((2, 256, 1024), bf16),
            V((2, 3, 256, 256), bf16),
            V((2, 3, 256, 256), bf16),
            V((2, 256, 256), f32),
            V((2, 3, 64, 256), bf16),
            V((2, 3, 64, 256), bf16),
            V((2, 64, 1024), f32),
            V((2, 3, 16, 1024), f32),
            V((256, 1024), f32),
            V((8, 2, 32, 128), f32),
            V((8, 2, 32, 128), bf16),
            V((NG - 1, 2, 32, 128), bf16),
            S((2, 2, 4)), S((2, 2, 4)),
            S((8,)), S((8,)),
            S((8,)), S((8,)),
            S((8,)), S((8,)),
            S((8,)), S((8,)),
            S((8, 4)), S((8, 4)),
            S((5,)), S((5,)),
        ],
        compiler_params=pltpu.CompilerParams(
            collective_id=0, has_side_effects=True, vmem_limit_bytes=48 * 1024 * 1024
        ),
    )(tokens, cotangents, left_root, right_root)
    new_left = stat_decay * left_stat + (1.0 - stat_decay) * gram_left
    new_right = stat_decay * right_stat + (1.0 - stat_decay) * gram_right
    new_momentum = momentum_decay * momentum + update
    return (new_left, new_right, new_momentum)


def solution(mesh):
    return jax.shard_map(
        shards,
        mesh=mesh,
        in_specs=(
            P("dp", "grid"),
            P(None, "dp", "tensor"),
            P(None, ("dp", "tensor"), "grid"),
            P(None, ("dp", "tensor"), "grid"),
            P(None, ("dp", "tensor"), "grid"),
            P(None, "grid", None),
            P(None, ("dp", "tensor", "grid"), None),
        ),
        out_specs=(
            P(None, ("dp", "tensor"), "grid"),
            P(None, ("dp", "tensor"), "grid"),
            P(None, ("dp", "tensor", "grid"), None),
        ),
        check_vma=False,
    )
```

time: 375 us -> 103 us (0.27)
  waiting for transfers between devices: 259 us -> 0 us
  Pallas kernels: 0 us -> 95 us
  blocking collectives: 46.6 us -> 0 us
  starting transfers between devices: 23.9 us -> 0 us
  between operations: 14 us -> 0.68 us
  matrix products: 10.4 us -> 0 us
  other arithmetic: 9.07 us -> 2.51 us
  local copies, waits for them, and re-layouts: 10.7 us -> 4.27 us
    all_gather x3 -> x0, waiting for transfers between devices: 146 us -> none  [the longest x1 58.3 us: spread(): lax.all_gather(own, axis, axis=0, tiled=True)[:len(lines)]]
    reduce_scatter x1 -> x0, waiting for transfers between devices: 110 us -> none  [spread(): own = lax.psum_scatter(padded, axis, scatter_dimension=0, tiled=True)]
    pallas_call x0 -> x1, Pallas kernels: none -> 95 us  [shards(): pl.pallas_call(kernel, out_shape=(jax.ShapeDtypeStruct((2, 256, 512), f32...]
    all_to_all x1 -> x0, blocking collectives: 37.9 us -> none  [sum_at_owner(): pieces = lax.all_to_all(in_blocks(shard, dim, size), axis, 0, 0, tiled=True)]
    all_to_all x3 -> x0, starting transfers between devices: 23.7 us -> none  [the longest x2 18.3 us: sum_at_owner(): pieces = lax.all_to_all(in_blocks(shard, dim, size), axis, 0, 0, tiled=True)]
    dot_general x5 -> x0, matrix products: 10.4 us -> none  [the longest x1 3.3 us: shards(): jnp.einsum('pak,pbk->pab', own_rows, grad_rows, preferred_element_type=jn...]
    all_gather x1 -> x0, blocking collectives: 8.74 us -> none  [shards(): lax.all_gather(shared.astype(jnp.bfloat16), 'tensor', axis=2, tiled=True)]
  transfers between devices with their start and end apart: 7 -> 0, of which waited for: 5 -> 0; matrix products, arithmetic and copies ran while one was open for 6% -> 0% of each run, Pallas kernels for 0% -> 0%
where the time goes in v1:
time: 103 us; the launch traced here: 102 us
  Pallas kernels  95 us (92%)
  local copies, waits for them, and re-layouts  4.27 us (4%)
  other arithmetic  2.51 us (2%)
    pallas_call x1, Pallas kernels, shards(): pl.pallas_call(kernel, out_shape=(jax.ShapeDtypeStruct((2, 256, 512), f32...  95 us
    unnamed x14, local copies, waits for them, and re-layouts  4.27 us

profile of v1, /device:TPU:1, one launch (start us, length us, event | category | flops | bytes accessed | tf_op | source)
XLA Modules:
  0.0 102.4 jit_solution(11102092909537749118)
XLA Ops:
  0.6 0.0 copy-start
  0.6 1.1 %copy-done = bf16[768,512]{1,0:T(8,128)(2,1)S(1)} copy-done((bf16[768,512]{1,0:T(8,128)(2,1)S(1)}, bf16[768,512]{1,0:T(8,128)(2,1)}, u32[]{:S(2)}) %copy-start) | copy-done | bytes 786456
  1.8 0.0 copy-start.1
  1.8 1.1 %copy-done.1 = bf16[2,768,256]{2,1,0:T(8,128)(2,1)S(1)} copy-done((bf16[2,768,256]{2,1,0:T(8,128)(2,1)S(1)}, bf16[2,768,256]{2,1,0:T(8,128)(2,1)}, u32[]{:S(2)}) %copy-start.1) | copy-done | bytes 786456
  2.9 0.0 copy-start.2
  2.9 1.0 %copy-done.2 = bf16[2,256,512]{2,1,0:T(8,128)(2,1)S(1)} copy-done((bf16[2,256,512]{2,1,0:T(8,128)(2,1)S(1)}, bf16[2,256,512]{2,1,0:T(8,128)(2,1)}, u32[]{:S(2)}) %copy-start.2) | copy-done | bytes 524312
  3.9 0.0 copy-start.3
  3.9 0.9 copy-done.3
  4.9 0.0 copy-start.4
  4.9 95.0 %shard_map.94 = (f32[2,256,512]{2,1,0:T(8,128)S(1)}, f32[2,32,64]{2,1,0:T(8,128)S(1)}, f32[2,16,1024]{2,1,0:T(8,128)S(1)}) custom-call(bf16[768,512]{1,0:T(8,128)(2,1)S(1)} %copy-done, bf16[2,768,256]{2,1,0:T(8,128)(2,1)S(1)} %copy-done.1, bf16[2,256,512]{2,1,0:T(8,128)(2,1)S(1)} %copy-done.2, bf16[2,64,1024]{2,1,0:T(8,128)(2,1)S(1)} %copy-done.3), custom_call_target="tpu_custom_call" | custom-call | tf_op jit(solution)/shard_map/pallas_call | solution.py:322
  99.9 0.0 copy-done.4
  99.9 0.0 copy-start.6
  99.9 0.0 copy-start.5
  99.9 1.2 %multiply_add_fusion = f32[2,256,512]{2,1,0:T(8,128)} fusion(f32[2,256,512]{2,1,0:T(8,128)S(1)} %get-tuple-element.6, f32[2,256,512]{2,1,0:T(8,128)S(1)} %copy-done.4), kind=kLoop, calls=%fused_computation | loop fusion | flops 786432 | bytes 3145728 | tf_op jit(solution)/shard_map/add | solution.py:364
  101.1 0.0 copy-done.6
  101.1 0.6 multiply_add_fusion.2
  101.7 0.0 copy-done.5
  101.7 0.7 multiply_add_fusion.1
Async XLA Ops:
  0.6 1.1 %copy-start = (bf16[768,512]{1,0:T(8,128)(2,1)S(1)}, bf16[768,512]{1,0:T(8,128)(2,1)}, u32[]{:S(2)}) copy-start(bf16[768,512]{1,0:T(8,128)(2,1)} %tokens.1) | copy-start | bytes 2359300
  1.8 1.1 %copy-start.1 = (bf16[2,768,256]{2,1,0:T(8,128)(2,1)S(1)}, bf16[2,768,256]{2,1,0:T(8,128)(2,1)}, u32[]{:S(2)}) copy-start(bf16[2,768,256]{2,1,0:T(8,128)(2,1)} %cots.1) | copy-start | bytes 2359300
  2.9 1.0 %copy-start.2 = (bf16[2,256,512]{2,1,0:T(8,128)(2,1)S(1)}, bf16[2,256,512]{2,1,0:T(8,128)(2,1)}, u32[]{:S(2)}) copy-start(bf16[2,256,512]{2,1,0:T(8,128)(2,1)} %left_root.1) | copy-start | bytes 1572868
  3.9 0.9 copy-start.3
  4.9 95.0 %copy-start.4 = (f32[2,256,512]{2,1,0:T(8,128)S(1)}, f32[2,256,512]{2,1,0:T(8,128)}, u32[]{:S(2)}) copy-start(f32[2,256,512]{2,1,0:T(8,128)} %param.9) | copy-start | bytes 3145732
  99.9 1.2 %copy-start.6 = (f32[2,32,64]{2,1,0:T(8,128)S(1)}, f32[2,32,64]{2,1,0:T(8,128)}, u32[]{:S(2)}) copy-start(f32[2,32,64]{2,1,0:T(8,128)} %param.10) | copy-start | bytes 49156
  99.9 1.9 %copy-start.5 = (f32[2,16,1024]{2,1,0:T(8,128)S(1)}, f32[2,16,1024]{2,1,0:T(8,128)}, u32[]{:S(2)}) copy-start(f32[2,16,1024]{2,1,0:T(8,128)} %param.13) | copy-start | bytes 393220

commit v2 on v1

v2 whole, which is shorter than its diff:
```python
import jax
import jax.numpy as jnp
from jax import lax
from jax.experimental import pallas as pl
from jax.experimental.pallas import tpu as pltpu
from jax.sharding import PartitionSpec as P

MESH = pl.DeviceIdType.MESH
f32, bf16 = jnp.float32, jnp.bfloat16

stat_decay = 0.9
momentum_decay = 0.9

NZ, NT, NG, NX, NY = 8, 4, 16, 4, 4
Z_ORDER = (1, 7, 2, 6, 3, 5, 4, 8)


def remote(src, dst, send_sem, recv_sem, device):
    return pltpu.make_async_remote_copy(
        src_ref=src, dst_ref=dst, send_sem=send_sem, recv_sem=recv_sem,
        device_id=device, device_id_type=MESH,
    )


def kernel(
    tokens_hbm, cots_hbm, left_root_hbm, right_root_hbm,
    gram_left, gram_right, update,
    tokens, cots, lr, right_root,
    part, ring, gbuf, gsub, r2, r3, rbuf, rr,
    xs, xr, ax, ys, yr, uf, ur, gr_tmp, gs32, gs, gr, gl,
    ring_send, ring_recv, ag_send, ag_recv, sib_send, sib_recv, yl_send, yl_recv,
    sib2_send, sib2_recv, x_send, x_recv, pair_send, pair_recv, in_sem,
    lr_send, lr_recv, rr_send, rr_recv,
):
    d, t, g = lax.axis_index("dp"), lax.axis_index("tensor"), lax.axis_index("grid")
    y, x = g // NX, g % NX
    core, y_lo = t % 2, t // 2
    sibling = y_lo * 2 + (1 - core)
    partner = (1 - y_lo) * 2 + core
    across = (1 - y_lo) * 2 + 1 - core
    learner = d * NT + t

    loads = [
        pltpu.make_async_copy(src, dst, in_sem.at[i])
        for i, (src, dst) in enumerate(
            ((tokens_hbm, tokens), (cots_hbm, cots), (right_root_hbm, right_root), (left_root_hbm, lr.at[:, t]))
        )
    ]
    for load in loads:
        load.start()

    barrier = pltpu.get_barrier_semaphore()

    def greet(*device):
        pl.semaphore_signal(barrier, inc=1, device_id=device, device_id_type=MESH)

    rows_z, rows_t = g // 2, (g % 2) * 2 + d // 4
    mine = jnp.logical_and(rows_z == d, rows_t == t)
    source_g = 2 * d + y_lo

    @pl.loop(1, NZ)
    def _(k):
        greet((d + k) % NZ, t, g)

    greet(d, sibling, g)
    greet(d, partner, g)
    greet(d, across, g)

    @pl.loop(0, 16)
    def _(k):
        z, other = core * 4 + k // NT, k % NT

        @pl.when(jnp.logical_or(jnp.logical_or(z != d, other != t), source_g != g))
        def _():
            greet(z, other, source_g)

    @pl.loop(1, NG)
    def _(k):
        greet(d, t, (g + k) % NG)

    loads[0].wait()
    loads[1].wait()
    turned = tokens[...].T
    for p in range(2):
        whole = jnp.dot(turned, cots[p], preferred_element_type=f32)
        for z in range(NZ):
            part[z, p] = whole[z * 64 : z * 64 + 64]

    pl.semaphore_wait(barrier, NZ - 1 + 3 + NG - 1 + jnp.where(mine, 15, 16))

    loads[2].wait()

    sent = []

    def go(copy):
        copy.start()
        sent.append(copy)

    loads[3].wait()
    go(remote(lr.at[:, t], lr.at[:, t], lr_send.at[0], lr_recv.at[0], (d, partner, g)))
    go(remote(lr.at[:, t], lr.at[:, t], lr_send.at[1], lr_recv.at[1], (d, sibling, g)))

    def own_root(where):
        return rr.at[:, pl.ds(where * 64, 64), :]

    @pl.when(y == t)
    def _():
        for k in (2, 1, 3):
            remote(right_root, own_root(x), rr_send.at[k], rr_recv.at[0], (d, t, ((y + k) % NY) * NX + x)).start()
        rr[:, pl.ds(x * 64, 64), :] = right_root[...]

    up, down = ((d + 1) % NZ, t, g), ((d + NZ - 1) % NZ, t, g)

    def length(way, stream):
        return 4 if way == stream % 2 else 3

    STREAMS = ((0, 0, 0), (1, 1, 0), (2, 1, 1), (3, 0, 1))

    for step in range(4):
        for stream, p, half in STREAMS:
            rows = slice(half * 32, half * 32 + 32)
            for way in range(2):
                n = length(way, stream)
                if step >= n:
                    continue
                e = (d + n - step) % NZ if way == 0 else (d + NZ - n + step) % NZ
                if step == 0:
                    src = part.at[e, p, rows]
                else:
                    last = (way, stream, step - 1)
                    src = ring.at[last]
                    remote(src, src, ring_send.at[last], ring_recv.at[last], up).wait_recv()
                    ring[last] = ring[last] + part[e, p, rows]
                this = (way, stream, step)
                go(remote(src, ring.at[this], ring_send.at[this], ring_recv.at[this], up if way == 0 else down))
    for stream, p, half in STREAMS:
        total = part[d, p, half * 32 : half * 32 + 32]
        for way in range(2):
            last = (way, stream, length(way, stream) - 1)
            slot = ring.at[last]
            remote(slot, slot, ring_send.at[last], ring_recv.at[last], up).wait_recv()
            total = total + ring[last]
        piece = total.astype(bf16)
        gbuf[p, t, pl.ds(d * 64 + half * 32, 32), :] = piece
        for a in range(2):
            for c in range(2):
                gsub[p * 8 + (half * 2 + a) * 2 + c] = piece[a * 16 : a * 16 + 16, c * 128 : c * 128 + 128]

    def rows_of(tensor, k):
        rows = pl.ds(((d + NZ - k) % NZ) * 64, 64)
        if k in (4, 8):
            return gbuf.at[k // 4 - 1, tensor, pl.ds(((d + 4) % NZ) * 64, 64), :]
        return gbuf.at[:, tensor, rows, :]

    def along(src, k, to):
        go(remote(src, src, ag_send.at[k], ag_recv.at[k], (to % NZ, t, g)))

    along(rows_of(t, 0), 2, d + 2)
    along(rows_of(t, 0), 6, d + 6)
    along(rows_of(t, 0), 1, d + 1)
    along(rows_of(t, 0), 7, d + 7)

    def pass_on(k):
        go(remote(rows_of(t, k), rows_of(t, k), yl_send.at[k], yl_recv.at[k], (d, partner, g)))
        go(remote(rows_of(t, k), rows_of(t, k), sib_send.at[k], sib_recv.at[k], (d, sibling, g)))

    def pass_again(k):
        here = rows_of(partner, k)
        remote(here, here, yl_send.at[k], yl_recv.at[k], (d, partner, g)).wait_recv()
        go(remote(here, here, sib2_send.at[k], sib2_recv.at[k], (d, sibling, g)))

    def arrived(k):
        here = rows_of(t, k)
        remote(here, here, ag_send.at[k], ag_recv.at[k], (d, partner, g)).wait_recv()

    pass_on(0)

    def many(ref, s):
        return remote(ref, ref, pair_send.at[s], pair_recv.at[s], (d, sibling, g))

    @pl.loop(0, NG)
    def _(k):
        @pl.when(jnp.logical_or(jnp.logical_not(mine), k != g))
        def _():
            remote(gsub.at[k], r2.at[(d % 4) * NT + t], pair_send.at[1], pair_recv.at[1], (rows_z, rows_t, k)).start()

    @pl.when(mine)
    def _():
        r2[(d % 4) * NT + t] = gsub[g]

    def two_back(tensor, k, p):
        return gbuf.at[p, tensor, pl.ds(((d + NZ - k) % NZ) * 64, 64), :]

    arrived(2)
    along(two_back(t, 2, 0), 4, d + 2)
    along(rows_of(t, 2), 3, d + 1)
    arrived(6)
    along(two_back(t, 6, 1), 8, d + 6)
    along(rows_of(t, 6), 5, d + 7)
    for k in (2, 6, 1, 7):
        if k in (1, 7):
            arrived(k)
        pass_on(k)

    def lr_arrived(tensor, i):
        here = lr.at[:, tensor]
        remote(here, here, lr_send.at[i], lr_recv.at[i], (d, sibling, g)).wait_recv()

    lr_arrived(partner, 0)
    go(remote(lr.at[:, partner], lr.at[:, partner], lr_send.at[2], lr_recv.at[2], (d, sibling, g)))

    @pl.when(y != t)
    def _():
        remote(own_root(x), own_root(x), rr_send.at[0], rr_recv.at[0], (d, sibling, g)).wait_recv()

    for k in (2, 1, 3):
        go(remote(own_root(x), own_root(x), x_send.at[8, k], x_recv.at[8, k], (d, t, y * NX + (x + k) % NX)))

    @pl.when(mine)
    def _():
        many(r2.at[pl.ds(0, 15)], 1).wait_recv()

    @pl.when(jnp.logical_not(mine))
    def _():
        many(r2, 1).wait_recv()

    for k in range(1, NY):
        go(remote(r2, r3.at[x, y], x_send.at[0, k], x_recv.at[0, k], (d, t, ((y + k) % NY) * NX + x)))
    r3[x, y] = r2[...]

    lr_arrived(sibling, 1)
    lr_arrived(across, 2)
    for k in (3, 5, 4, 8):
        arrived(k)
        pass_on(k)

    def applied(p, at):
        rows = jnp.concatenate(
            [lr[p, i, pl.ds(q * 64 + at * 16, 16), :] for q in range(NY) for i in range(NT)], axis=0
        )
        return jnp.dot(rows, gbuf[p, t], preferred_element_type=f32)

    for p in range(2):
        for k in (2, 1, 3):
            xs[p, k - 1] = applied(p, (x + k) % NX).astype(bf16)
            go(remote(xs.at[p, k - 1], xr.at[p, k - 1], x_send.at[2 + p, k], x_recv.at[2 + p, k],
                      (d, t, y * NX + (x + k) % NX)))
        ax[p] = applied(p, x)

    for k in (0,) + Z_ORDER:
        pass_again(k)

    for k in range(1, NY):
        here = r3.at[x, (y + NY - k) % NY]
        remote(here, here, x_send.at[0, k], x_recv.at[0, k], (d, sibling, g)).wait_recv()
    for k in (2, 1, 3):
        go(remote(r3.at[x], r3.at[x], x_send.at[1, k], x_recv.at[1, k], (d, t, y * NX + (x + k) % NX)))

    for p in range(2):
        total = ax[p]
        for k in (1, 3, 2):
            here = xr.at[p, k - 1]
            remote(here, here, x_send.at[2 + p, k], x_recv.at[2 + p, k], (d, sibling, g)).wait_recv()
            total = total + xr[p, k - 1].astype(f32)
        ax[p] = total
        for k in (2, 1, 3):
            to = (y + k) % NY
            ys[p, k - 1] = ax[p, pl.ds(to * 64, 64), :].astype(bf16)
            go(remote(ys.at[p, k - 1], yr.at[p, k - 1], x_send.at[4 + p, k], x_recv.at[4 + p, k], (d, t, to * NX + x)))

    for k in (0,) + Z_ORDER:
        for tensor, sends, recvs in ((sibling, sib_send, sib_recv), (across, sib2_send, sib2_recv)):
            here = rows_of(tensor, k)
            remote(here, here, sends.at[k], recvs.at[k], (d, sibling, g)).wait_recv()

    for p in range(2):
        chosen = gbuf[p, d // 2].T
        for j in range(NT):
            gr_tmp[:, j * 256 : j * 256 + 256] = jnp.dot(chosen, gbuf[p, j], preferred_element_type=f32)
        lines = gr_tmp[pl.ds((learner % 8) * 32, 32), :]
        for c in range(8):
            block = lines[:, c * 128 : c * 128 + 128]
            gs32[c, p] = block
            gs[c, p] = block.astype(bf16)

    @pl.loop(1, NG)
    def _(k):
        to = (g + k) % NG
        remote(gs.at[to // 2], gr.at[k - 1], pair_send.at[4], pair_recv.at[4], (d, t, to)).start()

    def own_rows_ready():
        for k in (1, 3, 2):
            here = r3.at[(x + NX - k) % NX]
            remote(here, here, x_send.at[1, k], x_recv.at[1, k], (d, sibling, g)).wait_recv()
        for a in range(NX):
            for b in range(NY):
                p, rows, c = b // 2, (b % 2) * 2 + a // 2, a % 2
                for j in range(NT):
                    for z in range(4):
                        rbuf[p, j, z * 64 + rows * 16 : z * 64 + rows * 16 + 16, c * 128 : c * 128 + 128] = r3[a, b, z * NT + j]

    stores = [pltpu.make_async_copy(gl.at[p], gram_left.at[p], in_sem.at[4 + p]) for p in range(2)]

    def left(p):
        total = None
        for j in range(NT):
            term = lax.dot_general(rbuf[p, j], gbuf[p, j], (((1,), (1,)), ((), ())), preferred_element_type=f32)
            total = term if total is None else total + term
        gl[p] = total
        stores[p].start()

    for k in (1, 3, 2):
        here = own_root((x + NX - k) % NX)
        remote(here, here, x_send.at[8, k], x_recv.at[8, k], (d, sibling, g)).wait_recv()

    TENSOR = ((1, sibling), (2, partner), (3, across))

    for p in range(2):
        total = ax[p, pl.ds(y * 64, 64), :]
        for k in (1, 3, 2):
            here = yr.at[p, k - 1]
            remote(here, here, x_send.at[4 + p, k], x_recv.at[4 + p, k], (d, sibling, g)).wait_recv()
            total = total + yr[p, k - 1].astype(f32)
        high = total.astype(bf16)
        rest = total - high.astype(f32)
        middle = rest.astype(bf16)
        low = (rest - middle.astype(f32)).astype(bf16)
        product = jnp.dot(jnp.concatenate([high, middle, low]), rr[p], preferred_element_type=f32)
        uf[p] = product[:64] + (product[64:128] + product[128:])
        for k, to in reversed(TENSOR):
            go(remote(uf.at[p, pl.ds(to * 16, 16)], ur.at[p, k - 1], x_send.at[6 + p, k], x_recv.at[6 + p, k], (d, to, g)))

    many(gr, 4).wait_recv()
    for p in range(2):
        total = gs32[g // 2, p]
        for k in range(NG - 1):
            total = total + gr[k, p].astype(f32)
        gram_right[p] = jnp.where(g % 2 == 0, total[:, :64], total[:, 64:])

    own_rows_ready()
    left(0)
    left(1)

    for p in range(2):
        total = uf[p, pl.ds(t * 16, 16), :]
        for k in (1, 3, 2):
            here = ur.at[p, k - 1]
            remote(here, here, x_send.at[6 + p, k], x_recv.at[6 + p, k], (d, sibling, g)).wait_recv()
            total = total + ur[p, k - 1]
        update[p] = total

    for store in stores:
        store.wait()
    for copy in sent:
        copy.wait_send()
    many(gr, 4).wait_send()

    @pl.when(mine)
    def _():
        many(r2.at[pl.ds(0, 15)], 1).wait_send()

    @pl.when(jnp.logical_not(mine))
    def _():
        many(r2, 1).wait_send()

    @pl.when(y == t)
    def _():
        for k in (2, 1, 3):
            remote(right_root, own_root(x), rr_send.at[k], rr_recv.at[0], (d, sibling, g)).wait_send()


def shards(tokens, cotangents, left_stat, right_stat, left_root, right_root, momentum):
    vmem = pl.BlockSpec(memory_space=pltpu.VMEM)
    V, S = pltpu.VMEM, pltpu.SemaphoreType.DMA
    gram_left, gram_right, update = pl.pallas_call(
        kernel,
        out_shape=(
            jax.ShapeDtypeStruct((2, 256, 512), f32),
            jax.ShapeDtypeStruct((2, 32, 64), f32),
            jax.ShapeDtypeStruct((2, 16, 1024), f32),
        ),
        in_specs=[pl.BlockSpec(memory_space=pltpu.HBM)] * 4,
        out_specs=(pl.BlockSpec(memory_space=pltpu.HBM), vmem, vmem),
        scratch_shapes=[
            V(tokens.shape, bf16),
            V(cotangents.shape, bf16),
            V((2, NT, 256, 512), bf16),
            V(right_root.shape, bf16),
            V((NZ, 2, 64, 256), f32),
            V((2, 4, 4, 32, 256), f32),
            V((2, NT, 512, 256), bf16),
            V((NG, 16, 128), bf16),
            V((16, 16, 128), bf16),
            V((NX, NY, 16, 16, 128), bf16),
            V((2, NT, 256, 256), bf16),
            V((2, 256, 1024), bf16),
            V((2, 3, 256, 256), bf16),
            V((2, 3, 256, 256), bf16),
            V((2, 256, 256), f32),
            V((2, 3, 64, 256), bf16),
            V((2, 3, 64, 256), bf16),
            V((2, 64, 1024), f32),
            V((2, 3, 16, 1024), f32),
            V((256, 1024), f32),
            V((8, 2, 32, 128), f32),
            V((8, 2, 32, 128), bf16),
            V((NG - 1, 2, 32, 128), bf16),
            V((2, 256, 512), f32),
            S((2, 4, 4)), S((2, 4, 4)),
            S((9,)), S((9,)),
            S((9,)), S((9,)),
            S((9,)), S((9,)),
            S((9,)), S((9,)),
            S((9, 4)), S((9, 4)),
            S((5,)), S((5,)),
            S((6,)),
            S((3,)), S((3,)),
            S((4,)), S((1,)),
        ],
        compiler_params=pltpu.CompilerParams(
            collective_id=0, has_side_effects=True, vmem_limit_bytes=60 * 1024 * 1024
        ),
    )(tokens, cotangents, left_root, right_root)
    new_left = stat_decay * left_stat + (1.0 - stat_decay) * gram_left
    new_right = stat_decay * right_stat + (1.0 - stat_decay) * gram_right
    new_momentum = momentum_decay * momentum + update
    return (new_left, new_right, new_momentum)


def solution(mesh):
    return jax.shard_map(
        shards,
        mesh=mesh,
        in_specs=(
            P("dp", "grid"),
            P(None, "dp", "tensor"),
            P(None, ("dp", "tensor"), "grid"),
            P(None, ("dp", "tensor"), "grid"),
            P(None, ("dp", "tensor"), "grid"),
            P(None, "grid", None),
            P(None, ("dp", "tensor", "grid"), None),
        ),
        out_specs=(
            P(None, ("dp", "tensor"), "grid"),
            P(None, ("dp", "tensor"), "grid"),
            P(None, ("dp", "tensor", "grid"), None),
        ),
        check_vma=False,
    )
```

time: 103 us -> 88 us (0.85)
  Pallas kernels: 95 us -> 83.4 us
  local copies, waits for them, and re-layouts: 4.27 us -> 0.03 us
  other arithmetic: 2.51 us -> 3.78 us
    pallas_call x1, Pallas kernels: 95 us -> 83.4 us  [shards(): pl.pallas_call(kernel, out_shape=(jax.ShapeDtypeStruct((2, 256, 512), f32...]
    unnamed x14 -> x10, local copies, waits for them, and re-layouts: 4.27 us -> 0.03 us
    add x1, other arithmetic: 1.22 us -> 2.48 us  [shards(): new_left = stat_decay * left_stat + (1.0 - stat_decay) * gram_left]
where the time goes in v2:
time: 88 us; the launch traced here: 87.9 us
  Pallas kernels  83.4 us (95%)
  other arithmetic  3.78 us (4%)
    pallas_call x1, Pallas kernels, shards(): pl.pallas_call(kernel, out_shape=(jax.ShapeDtypeStruct((2, 256, 512), f32...  83.4 us
    add x1, other arithmetic, shards(): new_left = stat_decay * left_stat + (1.0 - stat_decay) * gram_left  2.48 us

profile of v2, /device:TPU:1, one launch (start us, length us, event | category | flops | bytes accessed | tf_op | source)
XLA Modules:
  0.0 87.9 jit_solution(15523124953262995829)
XLA Ops:
  0.6 0.0 copy-start
  0.6 83.4 %shard_map.94 = (f32[2,256,512]{2,1,0:T(8,128)}, f32[2,32,64]{2,1,0:T(8,128)}, f32[2,16,1024]{2,1,0:T(8,128)}) custom-call(bf16[768,512]{1,0:T(8,128)(2,1)} %tokens_hbm.1, bf16[2,768,256]{2,1,0:T(8,128)(2,1)} %cots_hbm.1, bf16[2,256,512]{2,1,0:T(8,128)(2,1)} %left_root_hbm.1, bf16[2,64,1024]{2,1,0:T(8,128)(2,1)} %right_root_hbm.1), custom_call_target="tpu_custom_call" | custom-call | tf_op jit(solution)/shard_map/pallas_call | solution.py:375
  84.0 0.0 copy-done
  84.0 0.0 copy-start.3
  84.1 0.0 copy-start.4
  84.1 0.0 copy-start.1
  84.1 0.0 copy-start.2
  84.1 2.5 %multiply_add_fusion = f32[2,256,512]{2,1,0:T(8,128)} fusion(f32[2,256,512]{2,1,0:T(8,128)} %get-tuple-element.6, f32[2,256,512]{2,1,0:T(8,128)S(1)} %copy-done), kind=kLoop, calls=%fused_computation | loop fusion | flops 786432 | bytes 3145728 | tf_op jit(solution)/shard_map/add | solution.py:424
  86.6 0.0 copy-done.3
  86.6 0.0 copy-done.4
  86.6 0.6 multiply_add_fusion.2
  87.2 0.0 copy-done.1
  87.2 0.0 copy-done.2
  87.2 0.7 multiply_add_fusion.1
Async XLA Ops:
  0.6 83.4 %copy-start = (f32[2,256,512]{2,1,0:T(8,128)S(1)}, f32[2,256,512]{2,1,0:T(8,128)}, u32[]{:S(2)}) copy-start(f32[2,256,512]{2,1,0:T(8,128)} %param.9) | copy-start | bytes 3145732
  84.0 2.5 %copy-start.3 = (f32[2,32,64]{2,1,0:T(8,128)S(1)}, f32[2,32,64]{2,1,0:T(8,128)}, u32[]{:S(2)}) copy-start(f32[2,32,64]{2,1,0:T(8,128)} %param.10) | copy-start | bytes 49156
  84.1 2.5 %copy-start.4 = (f32[2,32,64]{2,1,0:T(8,128)S(1)}, f32[2,32,64]{2,1,0:T(8,128)}, u32[]{:S(2)}) copy-start(f32[2,32,64]{2,1,0:T(8,128)} %get-tuple-element.7) | copy-start | bytes 49156
  84.1 3.1 %copy-start.1 = (f32[2,16,1024]{2,1,0:T(8,128)S(1)}, f32[2,16,1024]{2,1,0:T(8,128)}, u32[]{:S(2)}) copy-start(f32[2,16,1024]{2,1,0:T(8,128)} %param.13) | copy-start | bytes 393220
  84.1 3.1 %copy-start.2 = (f32[2,16,1024]{2,1,0:T(8,128)S(1)}, f32[2,16,1024]{2,1,0:T(8,128)}, u32[]{:S(2)}) copy-start(f32[2,16,1024]{2,1,0:T(8,128)} %get-tuple-element.8) | copy-start | bytes 393220

commit v3 on v2

--- a/solution.py
+++ b/solution.py
@@ -12,7 +12,7 @@
 momentum_decay = 0.9
 
 NZ, NT, NG, NX, NY = 8, 4, 16, 4, 4
-Z_ORDER = (1, 7, 2, 6, 3, 5, 4, 8)
+Z_ORDER = (2, 6, 1, 7, 3, 5, 4)
 
 
 def remote(src, dst, send_sem, recv_sem, device):
@@ -96,10 +96,6 @@
         copy.start()
         sent.append(copy)
 
-    loads[3].wait()
-    go(remote(lr.at[:, t], lr.at[:, t], lr_send.at[0], lr_recv.at[0], (d, partner, g)))
-    go(remote(lr.at[:, t], lr.at[:, t], lr_send.at[1], lr_recv.at[1], (d, sibling, g)))
-
     def own_root(where):
         return rr.at[:, pl.ds(where * 64, 64), :]
 
@@ -133,32 +129,44 @@
                     ring[last] = ring[last] + part[e, p, rows]
                 this = (way, stream, step)
                 go(remote(src, ring.at[this], ring_send.at[this], ring_recv.at[this], up if way == 0 else down))
-    for stream, p, half in STREAMS:
-        total = part[d, p, half * 32 : half * 32 + 32]
-        for way in range(2):
-            last = (way, stream, length(way, stream) - 1)
-            slot = ring.at[last]
-            remote(slot, slot, ring_send.at[last], ring_recv.at[last], up).wait_recv()
-            total = total + ring[last]
-        piece = total.astype(bf16)
-        gbuf[p, t, pl.ds(d * 64 + half * 32, 32), :] = piece
-        for a in range(2):
-            for c in range(2):
-                gsub[p * 8 + (half * 2 + a) * 2 + c] = piece[a * 16 : a * 16 + 16, c * 128 : c * 128 + 128]
+        if step == 1:
+            loads[3].wait()
+            go(remote(lr.at[:, t], lr.at[:, t], lr_send.at[0], lr_recv.at[0], (d, partner, g)))
+            go(remote(lr.at[:, t], lr.at[:, t], lr_send.at[1], lr_recv.at[1], (d, sibling, g)))
 
     def rows_of(tensor, k):
-        rows = pl.ds(((d + NZ - k) % NZ) * 64, 64)
-        if k in (4, 8):
-            return gbuf.at[k // 4 - 1, tensor, pl.ds(((d + 4) % NZ) * 64, 64), :]
-        return gbuf.at[:, tensor, rows, :]
-
-    def along(src, k, to):
-        go(remote(src, src, ag_send.at[k], ag_recv.at[k], (to % NZ, t, g)))
-
-    along(rows_of(t, 0), 2, d + 2)
-    along(rows_of(t, 0), 6, d + 6)
-    along(rows_of(t, 0), 1, d + 1)
-    along(rows_of(t, 0), 7, d + 7)
+        return gbuf.at[:, tensor, pl.ds(((d + NZ - k) % NZ) * 64, 64), :]
+
+    def half_of(p, tensor, k):
+        return gbuf.at[p, tensor, pl.ds(((d + NZ - k) % NZ) * 64, 64), :]
+
+    def along(p, k, to, arrives):
+        here = half_of(p, t, k)
+        go(remote(here, here, ag_send.at[p, arrives], ag_recv.at[p, arrives], (to % NZ, t, g)))
+
+    def arrived(p, k):
+        here = half_of(p, t, k)
+        remote(here, here, ag_send.at[p, k], ag_recv.at[p, k], (d, partner, g)).wait_recv()
+
+    for q in range(2):
+        for stream, p, half in STREAMS:
+            if p != q:
+                continue
+            total = part[d, p, half * 32 : half * 32 + 32]
+            for way in range(2):
+                last = (way, stream, length(way, stream) - 1)
+                slot = ring.at[last]
+                remote(slot, slot, ring_send.at[last], ring_recv.at[last], up).wait_recv()
+                total = total + ring[last]
+            piece = total.astype(bf16)
+            gbuf[p, t, pl.ds(d * 64 + half * 32, 32), :] = piece
+            for a in range(2):
+                for c in range(2):
+                    gsub[p * 8 + (half * 2 + a) * 2 + c] = piece[a * 16 : a * 16 + 16, c * 128 : c * 128 + 128]
+        along(q, 0, d + 2, 2)
+        along(q, 0, d + 6, 6)
+        along(q, 0, d + 1, 1)
+        along(q, 0, d + 7, 7)
 
     def pass_on(k):
         go(remote(rows_of(t, k), rows_of(t, k), yl_send.at[k], yl_recv.at[k], (d, partner, g)))
@@ -168,12 +176,6 @@
         here = rows_of(partner, k)
         remote(here, here, yl_send.at[k], yl_recv.at[k], (d, partner, g)).wait_recv()
         go(remote(here, here, sib2_send.at[k], sib2_recv.at[k], (d, sibling, g)))
-
-    def arrived(k):
-        here = rows_of(t, k)
-        remote(here, here, ag_send.at[k], ag_recv.at[k], (d, partner, g)).wait_recv()
-
-    pass_on(0)
 
     def many(ref, s):
         return remote(ref, ref, pair_send.at[s], pair_recv.at[s], (d, sibling, g))
@@ -188,33 +190,51 @@
     def _():
         r2[(d % 4) * NT + t] = gsub[g]
 
-    def two_back(tensor, k, p):
-        return gbuf.at[p, tensor, pl.ds(((d + NZ - k) % NZ) * 64, 64), :]
-
-    arrived(2)
-    along(two_back(t, 2, 0), 4, d + 2)
-    along(rows_of(t, 2), 3, d + 1)
-    arrived(6)
-    along(two_back(t, 6, 1), 8, d + 6)
-    along(rows_of(t, 6), 5, d + 7)
-    for k in (2, 6, 1, 7):
-        if k in (1, 7):
-            arrived(k)
-        pass_on(k)
+    pass_on(0)
+
+    for p in range(2):
+        arrived(p, 2)
+        if p == 0:
+            along(p, 2, d + 2, 4)
+        along(p, 2, d + 1, 3)
+        arrived(p, 6)
+        if p == 1:
+            along(p, 6, d + 6, 4)
+        along(p, 6, d + 7, 5)
 
     def lr_arrived(tensor, i):
         here = lr.at[:, tensor]
         remote(here, here, lr_send.at[i], lr_recv.at[i], (d, sibling, g)).wait_recv()
 
+    def next_x(k):
+        return (d, t, y * NX + (x + k) % NX)
+
+    def spread_x(here, row):
+        for k in (1, 3):
+            go(remote(here(x), here(x), x_send.at[row, k], x_recv.at[row, k], next_x(k)))
+
+    def spread_on(here, part_of, row):
+        for k in (1, 3):
+            at = (x + NX - k) % NX
+            remote(here(at), here(at), x_send.at[row, k], x_recv.at[row, k], (d, sibling, g)).wait_recv()
+            half = part_of(k // 2, at)
+            go(remote(half, half, x_send.at[row, k - 1], x_recv.at[row, k - 1], next_x(k)))
+
+    def spread_done(part_of, row):
+        for k in (1, 3):
+            half = part_of(k // 2, (x + 2) % NX)
+            remote(half, half, x_send.at[row, k - 1], x_recv.at[row, k - 1], (d, sibling, g)).wait_recv()
+
+    def root_half(p, where):
+        return rr.at[p, pl.ds(where * 64, 64), :]
+
+    @pl.when(y != t)
+    def _():
+        remote(own_root(x), own_root(x), rr_send.at[0], rr_recv.at[0], (d, sibling, g)).wait_recv()
+
+    spread_x(own_root, 8)
     lr_arrived(partner, 0)
     go(remote(lr.at[:, partner], lr.at[:, partner], lr_send.at[2], lr_recv.at[2], (d, sibling, g)))
-
-    @pl.when(y != t)
-    def _():
-        remote(own_root(x), own_root(x), rr_send.at[0], rr_recv.at[0], (d, sibling, g)).wait_recv()
-
-    for k in (2, 1, 3):
-        go(remote(own_root(x), own_root(x), x_send.at[8, k], x_recv.at[8, k], (d, t, y * NX + (x + k) % NX)))
 
     @pl.when(mine)
     def _():
@@ -230,9 +250,6 @@
 
     lr_arrived(sibling, 1)
     lr_arrived(across, 2)
-    for k in (3, 5, 4, 8):
-        arrived(k)
-        pass_on(k)
 
     def applied(p, at):
         rows = jnp.concatenate(
@@ -241,22 +258,24 @@
         return jnp.dot(rows, gbuf[p, t], preferred_element_type=f32)
 
     for p in range(2):
+        for k in (1, 7, 3, 5, 4):
+            arrived(p, k)
         for k in (2, 1, 3):
             xs[p, k - 1] = applied(p, (x + k) % NX).astype(bf16)
-            go(remote(xs.at[p, k - 1], xr.at[p, k - 1], x_send.at[2 + p, k], x_recv.at[2 + p, k],
-                      (d, t, y * NX + (x + k) % NX)))
+            go(remote(xs.at[p, k - 1], xr.at[p, k - 1], x_send.at[2 + p, k], x_recv.at[2 + p, k], next_x(k)))
         ax[p] = applied(p, x)
 
-    for k in (0,) + Z_ORDER:
-        pass_again(k)
-
-    for k in range(1, NY):
-        here = r3.at[x, (y + NY - k) % NY]
-        remote(here, here, x_send.at[0, k], x_recv.at[0, k], (d, sibling, g)).wait_recv()
-    for k in (2, 1, 3):
-        go(remote(r3.at[x], r3.at[x], x_send.at[1, k], x_recv.at[1, k], (d, t, y * NX + (x + k) % NX)))
-
-    for p in range(2):
+    for k in Z_ORDER:
+        pass_on(k)
+    spread_on(own_root, root_half, 8)
+
+    def rows_at(where):
+        return r3.at[where]
+
+    def rows_half(half, where):
+        return r3.at[where, half * 2 : half * 2 + 2]
+
+    def sum_x(p):
         total = ax[p]
         for k in (1, 3, 2):
             here = xr.at[p, k - 1]
@@ -268,30 +287,15 @@
             ys[p, k - 1] = ax[p, pl.ds(to * 64, 64), :].astype(bf16)
             go(remote(ys.at[p, k - 1], yr.at[p, k - 1], x_send.at[4 + p, k], x_recv.at[4 + p, k], (d, t, to * NX + x)))
 
-    for k in (0,) + Z_ORDER:
-        for tensor, sends, recvs in ((sibling, sib_send, sib_recv), (across, sib2_send, sib2_recv)):
-            here = rows_of(tensor, k)
-            remote(here, here, sends.at[k], recvs.at[k], (d, sibling, g)).wait_recv()
-
-    for p in range(2):
-        chosen = gbuf[p, d // 2].T
-        for j in range(NT):
-            gr_tmp[:, j * 256 : j * 256 + 256] = jnp.dot(chosen, gbuf[p, j], preferred_element_type=f32)
-        lines = gr_tmp[pl.ds((learner % 8) * 32, 32), :]
-        for c in range(8):
-            block = lines[:, c * 128 : c * 128 + 128]
-            gs32[c, p] = block
-            gs[c, p] = block.astype(bf16)
-
-    @pl.loop(1, NG)
-    def _(k):
-        to = (g + k) % NG
-        remote(gs.at[to // 2], gr.at[k - 1], pair_send.at[4], pair_recv.at[4], (d, t, to)).start()
+    sum_x(0)
+    for k in range(1, NY):
+        here = r3.at[x, (y + NY - k) % NY]
+        remote(here, here, x_send.at[0, k], x_recv.at[0, k], (d, sibling, g)).wait_recv()
+    spread_x(rows_at, 1)
+    sum_x(1)
 
     def own_rows_ready():
-        for k in (1, 3, 2):
-            here = r3.at[(x + NX - k) % NX]
-            remote(here, here, x_send.at[1, k], x_recv.at[1, k], (d, sibling, g)).wait_recv()
+        spread_done(rows_half, 1)
         for a in range(NX):
             for b in range(NY):
                 p, rows, c = b // 2, (b % 2) * 2 + a // 2, a % 2
@@ -309,13 +313,11 @@
         gl[p] = total
         stores[p].start()
 
-    for k in (1, 3, 2):
-        here = own_root((x + NX - k) % NX)
-        remote(here, here, x_send.at[8, k], x_recv.at[8, k], (d, sibling, g)).wait_recv()
+    spread_done(root_half, 8)
 
     TENSOR = ((1, sibling), (2, partner), (3, across))
 
-    for p in range(2):
+    def finish(p):
         total = ax[p, pl.ds(y * 64, 64), :]
         for k in (1, 3, 2):
             here = yr.at[p, k - 1]
@@ -330,16 +332,42 @@
         for k, to in reversed(TENSOR):
             go(remote(uf.at[p, pl.ds(to * 16, 16)], ur.at[p, k - 1], x_send.at[6 + p, k], x_recv.at[6 + p, k], (d, to, g)))
 
+    finish(0)
+    spread_on(rows_at, rows_half, 1)
+    for k in (0,) + Z_ORDER:
+        pass_again(k)
+    for k in (0,) + Z_ORDER:
+        for tensor, sends, recvs in ((sibling, sib_send, sib_recv), (across, sib2_send, sib2_recv)):
+            here = rows_of(tensor, k)
+            remote(here, here, sends.at[k], recvs.at[k], (d, sibling, g)).wait_recv()
+
+    for p in range(2):
+        chosen = gbuf[p, d // 2].T
+        for j in range(NT):
+            gr_tmp[:, j * 256 : j * 256 + 256] = jnp.dot(chosen, gbuf[p, j], preferred_element_type=f32)
+        lines = gr_tmp[pl.ds((learner % 8) * 32, 32), :]
+        for c in range(8):
+            block = lines[:, c * 128 : c * 128 + 128]
+            gs32[c, p] = block
+            gs[c, p] = block.astype(bf16)
+
+    @pl.loop(1, NG)
+    def _(k):
+        to = (g + k) % NG
+        remote(gs.at[to // 2], gr.at[k - 1], pair_send.at[4], pair_recv.at[4], (d, t, to)).start()
+
+    finish(1)
+
+    own_rows_ready()
+    left(0)
+    left(1)
+
     many(gr, 4).wait_recv()
     for p in range(2):
         total = gs32[g // 2, p]
         for k in range(NG - 1):
             total = total + gr[k, p].astype(f32)
         gram_right[p] = jnp.where(g % 2 == 0, total[:, :64], total[:, 64:])
-
-    own_rows_ready()
-    left(0)
-    left(1)
 
     for p in range(2):
         total = uf[p, pl.ds(t * 16, 16), :]
@@ -367,6 +395,12 @@
     def _():
         for k in (2, 1, 3):
             remote(right_root, own_root(x), rr_send.at[k], rr_recv.at[0], (d, sibling, g)).wait_send()
+
+
+def outputs(left_stat, gram_left, right_stat, gram_right, momentum, update, new_left, new_right, new_momentum):
+    new_left[...] = stat_decay * left_stat[...] + (1.0 - stat_decay) * gram_left[...]
+    new_right[...] = stat_decay * right_stat[...] + (1.0 - stat_decay) * gram_right[...]
+    new_momentum[...] = momentum_decay * momentum[...] + update[...]
 
 
 def shards(tokens, cotangents, left_stat, right_stat, left_root, right_root, momentum):
@@ -407,10 +441,10 @@
             V((NG - 1, 2, 32, 128), bf16),
             V((2, 256, 512), f32),
             S((2, 4, 4)), S((2, 4, 4)),
-            S((9,)), S((9,)),
-            S((9,)), S((9,)),
-            S((9,)), S((9,)),
-            S((9,)), S((9,)),
+            S((2, 8)), S((2, 8)),
+            S((8,)), S((8,)),
+            S((8,)), S((8,)),
+            S((8,)), S((8,)),
             S((9, 4)), S((9, 4)),
             S((5,)), S((5,)),
             S((6,)),
@@ -421,10 +455,16 @@
             collective_id=0, has_side_effects=True, vmem_limit_bytes=60 * 1024 * 1024
         ),
     )(tokens, cotangents, left_root, right_root)
-    new_left = stat_decay * left_stat + (1.0 - stat_decay) * gram_left
-    new_right = stat_decay * right_stat + (1.0 - stat_decay) * gram_right
-    new_momentum = momentum_decay * momentum + update
-    return (new_left, new_right, new_momentum)
+    arrays = (left_stat, gram_left, right_stat, gram_right, momentum, update)
+    blocks = [pl.BlockSpec((1, *array.shape[1:]), lambda p: (p, 0, 0)) for array in arrays]
+    return pl.pallas_call(
+        outputs,
+        grid=(2,),
+        out_shape=tuple(jax.ShapeDtypeStruct(array.shape, f32) for array in arrays[::2]),
+        in_specs=blocks,
+        out_specs=tuple(blocks[::2]),
+        name="outputs",
+    )(*arrays)
 
 
 def solution(mesh):

time: 88 us -> 84.4 us (0.959)
  other arithmetic: 3.78 us -> 0 us
    add x3 -> x0, other arithmetic: 3.78 us -> none  [the longest x1 2.48 us: shards(): new_left = stat_decay * left_stat + (1.0 - stat_decay) * gram_left]
    pallas_call x0 -> x1, Pallas kernels: none -> 2.55 us  [shards(): pl.pallas_call(outputs, grid=(2,), out_shape=tuple((jax.ShapeDtypeStruct(...]
    pallas_call x1, Pallas kernels: 83.4 us -> 81.1 us  [shards(): pl.pallas_call(kernel, out_shape=(jax.ShapeDtypeStruct((2, 256, 512), f32...]
where the time goes in v3:
time: 84.4 us; the launch traced here: 84.3 us
  Pallas kernels  83.6 us (99%)
    pallas_call x1, Pallas kernels, shards(): pl.pallas_call(kernel, out_shape=(jax.ShapeDtypeStruct((2, 256, 512), f32...  81.1 us
    pallas_call x1, Pallas kernels, shards(): pl.pallas_call(outputs, grid=(2,), out_shape=tuple((jax.ShapeDtypeStruct(...  2.55 us

profile of v3, /device:TPU:1, one launch (start us, length us, event | category | flops | bytes accessed | tf_op | source)
XLA Modules:
  0.0 84.3 jit_solution(14765525271835769406)
XLA Ops:
  0.6 81.1 %shard_map.94 = (f32[2,256,512]{2,1,0:T(8,128)}, f32[2,32,64]{2,1,0:T(8,128)}, f32[2,16,1024]{2,1,0:T(8,128)}) custom-call(bf16[768,512]{1,0:T(8,128)(2,1)} %tokens_hbm.1, bf16[2,768,256]{2,1,0:T(8,128)(2,1)} %cots_hbm.1, bf16[2,256,512]{2,1,0:T(8,128)(2,1)} %left_root_hbm.1, bf16[2,64,1024]{2,1,0:T(8,128)(2,1)} %right_root_hbm.1), custom_call_target="tpu_custom_call" | custom-call | tf_op jit(solution)/shard_map/pallas_call | solution.py:409
  81.7 2.6 %outputs.1 = (f32[2,256,512]{2,1,0:T(8,128)}, f32[2,32,64]{2,1,0:T(8,128)}, f32[2,16,1024]{2,1,0:T(8,128)}) custom-call(f32[2,256,512]{2,1,0:T(8,128)} %left_stat.1, f32[2,256,512]{2,1,0:T(8,128)} %get-tuple-element.6.gram_left, f32[2,32,64]{2,1,0:T(8,128)} %right_stat.1, f32[2,32,64]{2,1,0:T(8,128)} %get-tuple-element.7.gram_right, ...), custom_call_target="tpu_custom_call" | custom-call | tf_op jit(solution)/shard_map/outputs/pallas_call | solution.py:460

commit v4 on v3

--- a/solution.py
+++ b/solution.py
@@ -192,6 +192,34 @@
 
     pass_on(0)
 
+    def next_x(k):
+        return (d, t, y * NX + (x + k) % NX)
+
+    def spread_x(here, row):
+        for k in (1, 3):
+            go(remote(here(x), here(x), x_send.at[row, k], x_recv.at[row, k], next_x(k)))
+
+    def spread_on(here, part_of, row):
+        for k in (1, 3):
+            at = (x + NX - k) % NX
+            remote(here(at), here(at), x_send.at[row, k], x_recv.at[row, k], (d, sibling, g)).wait_recv()
+            half = part_of(k // 2, at)
+            go(remote(half, half, x_send.at[row, k - 1], x_recv.at[row, k - 1], next_x(k)))
+
+    def spread_done(part_of, row):
+        for k in (1, 3):
+            half = part_of(k // 2, (x + 2) % NX)
+            remote(half, half, x_send.at[row, k - 1], x_recv.at[row, k - 1], (d, sibling, g)).wait_recv()
+
+    def root_half(p, where):
+        return rr.at[p, pl.ds(where * 64, 64), :]
+
+    @pl.when(y != t)
+    def _():
+        remote(own_root(x), own_root(x), rr_send.at[0], rr_recv.at[0], (d, sibling, g)).wait_recv()
+
+    spread_x(own_root, 8)
+
     for p in range(2):
         arrived(p, 2)
         if p == 0:
@@ -202,37 +230,13 @@
             along(p, 6, d + 6, 4)
         along(p, 6, d + 7, 5)
 
+    for k in (2, 6):
+        pass_on(k)
+
     def lr_arrived(tensor, i):
         here = lr.at[:, tensor]
         remote(here, here, lr_send.at[i], lr_recv.at[i], (d, sibling, g)).wait_recv()
 
-    def next_x(k):
-        return (d, t, y * NX + (x + k) % NX)
-
-    def spread_x(here, row):
-        for k in (1, 3):
-            go(remote(here(x), here(x), x_send.at[row, k], x_recv.at[row, k], next_x(k)))
-
-    def spread_on(here, part_of, row):
-        for k in (1, 3):
-            at = (x + NX - k) % NX
-            remote(here(at), here(at), x_send.at[row, k], x_recv.at[row, k], (d, sibling, g)).wait_recv()
-            half = part_of(k // 2, at)
-            go(remote(half, half, x_send.at[row, k - 1], x_recv.at[row, k - 1], next_x(k)))
-
-    def spread_done(part_of, row):
-        for k in (1, 3):
-            half = part_of(k // 2, (x + 2) % NX)
-            remote(half, half, x_send.at[row, k - 1], x_recv.at[row, k - 1], (d, sibling, g)).wait_recv()
-
-    def root_half(p, where):
-        return rr.at[p, pl.ds(where * 64, 64), :]
-
-    @pl.when(y != t)
-    def _():
-        remote(own_root(x), own_root(x), rr_send.at[0], rr_recv.at[0], (d, sibling, g)).wait_recv()
-
-    spread_x(own_root, 8)
     lr_arrived(partner, 0)
     go(remote(lr.at[:, partner], lr.at[:, partner], lr_send.at[2], lr_recv.at[2], (d, sibling, g)))
 
@@ -265,7 +269,7 @@
             go(remote(xs.at[p, k - 1], xr.at[p, k - 1], x_send.at[2 + p, k], x_recv.at[2 + p, k], next_x(k)))
         ax[p] = applied(p, x)
 
-    for k in Z_ORDER:
+    for k in Z_ORDER[2:]:
         pass_on(k)
     spread_on(own_root, root_half, 8)
 
@@ -292,6 +296,8 @@
         here = r3.at[x, (y + NY - k) % NY]
         remote(here, here, x_send.at[0, k], x_recv.at[0, k], (d, sibling, g)).wait_recv()
     spread_x(rows_at, 1)
+    for k in (0,) + Z_ORDER:
+        pass_again(k)
     sum_x(1)
 
     def own_rows_ready():
@@ -332,10 +338,6 @@
         for k, to in reversed(TENSOR):
             go(remote(uf.at[p, pl.ds(to * 16, 16)], ur.at[p, k - 1], x_send.at[6 + p, k], x_recv.at[6 + p, k], (d, to, g)))
 
-    finish(0)
-    spread_on(rows_at, rows_half, 1)
-    for k in (0,) + Z_ORDER:
-        pass_again(k)
     for k in (0,) + Z_ORDER:
         for tensor, sends, recvs in ((sibling, sib_send, sib_recv), (across, sib2_send, sib2_recv)):
             here = rows_of(tensor, k)
@@ -356,7 +358,9 @@
         to = (g + k) % NG
         remote(gs.at[to // 2], gr.at[k - 1], pair_send.at[4], pair_recv.at[4], (d, t, to)).start()
 
+    finish(0)
     finish(1)
+    spread_on(rows_at, rows_half, 1)
 
     own_rows_ready()
     left(0)

time: 84.4 us -> 81.4 us (0.964)
  Pallas kernels: 83.6 us -> 80.2 us
    pallas_call x1, Pallas kernels: 81.1 us -> 77.7 us  [shards(): pl.pallas_call(kernel, out_shape=(jax.ShapeDtypeStruct((2, 256, 512), f32...]
where the time goes in v4:
time: 81.4 us; the launch traced here: 80.9 us
  Pallas kernels  80.2 us (99%)
    pallas_call x1, Pallas kernels, shards(): pl.pallas_call(kernel, out_shape=(jax.ShapeDtypeStruct((2, 256, 512), f32...  77.7 us
    pallas_call x1, Pallas kernels, shards(): pl.pallas_call(outputs, grid=(2,), out_shape=tuple((jax.ShapeDtypeStruct(...  2.55 us

profile of v4, /device:TPU:1, one launch (start us, length us, event | category | flops | bytes accessed | tf_op | source)
XLA Modules:
  0.0 80.9 jit_solution(34616910095986428)
XLA Ops:
  0.6 77.7 %shard_map.94 = (f32[2,256,512]{2,1,0:T(8,128)}, f32[2,32,64]{2,1,0:T(8,128)}, f32[2,16,1024]{2,1,0:T(8,128)}) custom-call(bf16[768,512]{1,0:T(8,128)(2,1)} %tokens_hbm.1, bf16[2,768,256]{2,1,0:T(8,128)(2,1)} %cots_hbm.1, bf16[2,256,512]{2,1,0:T(8,128)(2,1)} %left_root_hbm.1, bf16[2,64,1024]{2,1,0:T(8,128)(2,1)} %right_root_hbm.1), custom_call_target="tpu_custom_call" | custom-call | tf_op jit(solution)/shard_map/pallas_call | solution.py:413
  78.3 2.6 %outputs.1 = (f32[2,256,512]{2,1,0:T(8,128)}, f32[2,32,64]{2,1,0:T(8,128)}, f32[2,16,1024]{2,1,0:T(8,128)}) custom-call(f32[2,256,512]{2,1,0:T(8,128)} %left_stat.1, f32[2,256,512]{2,1,0:T(8,128)} %get-tuple-element.6.gram_left, f32[2,32,64]{2,1,0:T(8,128)} %right_stat.1, f32[2,32,64]{2,1,0:T(8,128)} %get-tuple-element.7.gram_right, ...), custom_call_target="tpu_custom_call" | custom-call | tf_op jit(solution)/shard_map/outputs/pallas_call | solution.py:464
